TPU v7x, 32 devices: a whole 2x2x4 slice. The times are simulated.
32 devices in a mesh: groups: 2 (over y), row: 4 (over z), col: 2 (over x), tok: 2 (over core).
Axes of the slice: x: 2, y: 2, z: 4, core: 2. Of those that a mesh axis runs over, the one named last changes fastest.
Arguments:
- tokens: bfloat16 [512, 8192], P(('groups', 'row', 'tok'), 'col'), parts along dimension 0, may hold values from -12 to 12
- up_weight: bfloat16 [8192, 32768], P('col', ('row', 'tok')), may hold values from -0.5 to 0.5
- block_mask: int32 [64, 256], P('col', ('row', 'tok')), may hold values from 0 to 1, as said below
Outputs:
- column_rms: float32 [65536], P(('groups', 'row', 'tok')), parts along dimension 0
There are 2 independent parts, one for each index of `groups`. A program takes and returns all parts, laid end to end along the dimension named above; an argument that names none is the same for every part. Nothing has to cross between parts.
Inputs may be any that keep to these rules, and one draw needn't show every extreme that they name: `block_mask`: in every block column, the block rows held by one index of col contain at most 24 ones, and some block column reaches 24; about half of all blocks are kept.
All inputs are finite; a program needn't handle non-finite values.
Results may differ from a plain program's by a relative error of at most 0.0003.
Values may be sent and summed in bfloat16 or wider, within the bound.
A program may use at most 256 MiB of HBM per device.

v0:
```python
import jax
import jax.numpy as jnp
from jax import lax
from jax.sharding import PartitionSpec as P

BLOCK = 128


def per_device(tokens, up_weight, block_mask):
    keep_mask = jnp.repeat(jnp.repeat(block_mask > 0, BLOCK, axis=0), BLOCK, axis=1)
    masked = jnp.where(keep_mask, up_weight, jnp.zeros_like(up_weight))
    partial_value = jnp.dot(
        lax.all_gather(tokens, ("row", "tok"), axis=0, tiled=True),
        masked,
        preferred_element_type=jnp.float32,
    )
    token_count = partial_value.shape[0]
    shares = lax.psum_scatter(partial_value, "col", scatter_dimension=0, tiled=True)
    activated = jax.nn.gelu(shares, approximate=False)
    local_sums = jnp.sum(activated * activated, axis=0)
    totals = lax.psum(local_sums, "col")
    return jnp.sqrt(totals / token_count + 1e-06)


def solution(mesh):
    placed = (
        P(("groups", "row", "tok"), "col"),
        P("col", ("row", "tok")),
        P("col", ("row", "tok")),
    )
    return jax.shard_map(
        per_device,
        mesh=mesh,
        in_specs=placed,
        out_specs=P(("groups", "row", "tok")),
        check_vma=False,
    )
```

profile of v0, /device:TPU:0, one launch (start us, length us, event | category | flops | bytes accessed | tf_op | source)
XLA Modules:
  0.0 164.9 jit_solution(11086052709999153271)
XLA Ops:
  6.5 0.0 all-gather.2.cloned.1.call-start
  6.5 0.7 all-gather.2.cloned.1.call-update
  7.3 0.0 reduce-scatter.2.cloned.1.call-start
  7.3 0.7 broadcast_compare_fusion
  8.0 32.8 %all-gather.2.cloned.1.call-done = bf16[256,4096]{1,0:T(8,128)(2,1)} async-done(((bf16[32,4096]{1,0:T(8,128)(2,1)}), bf16[256,4096]{1,0:T(8,128)(2,1)}) %all-gather.2.cloned.1.call-update) | async-done | bytes 2097168 | tf_op jit(solution)/shard_map/all_gather | solution.py:13
  40.8 0.1 broadcast_in_dim.9
  40.9 0.0 copy-start
  40.9 23.4 %broadcast_in_dim.10 = pred[4096,32,128]{2,1,0:T(32,128)(4,1)} broadcast(pred[4096,32]{1,0:T(8,128)(4,1)S(1)} %bitcast.11), dimensions={0,1} | broadcast | bytes 16908288 | tf_op jit(solution)/shard_map/broadcast_in_dim | solution.py:10
  64.4 0.0 copy-done
  64.4 26.2 %fusion.2 = f32[256,4096]{0,1:T(8,128)} fusion(bf16[256,4096]{1,0:T(8,128)(2,1)S(1)} %copy-done, bf16[4096,4096]{1,0:T(8,128)(2,1)} %param.4, pred[512,8,32,128]{3,2,1,0:T(32,128)(4,1)} %bitcast.10), kind=kOutput, calls=%fused_computation.3 | convolution fusion | flops 8606711808 | bytes 56623104 | tf_op jit(solution)/shard_map/dot_general | solution.py:12
  90.6 0.0 reduce-scatter.2.cloned.1.call-update
  90.6 53.9 %reduce-scatter.2.cloned.1.call-done = f32[128,4096]{0,1:T(8,128)} async-done(((f32[256,4096]{0,1:T(8,128)}), f32[128,4096]{0,1:T(8,128)}) %reduce-scatter.2.cloned.1.call-update) | async-done | bytes 2097168 | tf_op jit(solution)/shard_map/reduce_scatter | solution.py:18
  144.6 5.9 %fusion.6 = f32[4096]{0:T(1024)S(1)} fusion(f32[128,4096]{0,1:T(8,128)} %reduce-scatter.2.cloned.1.call-done), kind=kLoop, calls=%fused_computation.8 | loop fusion | flops 34598912 | bytes 2113536 | tf_op jit(solution)/shard_map/reduce_sum | solution.py:20
  150.5 7.0 %psum.7 = f32[4096]{0:T(1024)S(1)} all-reduce(f32[4096]{0:T(1024)S(1)} %fusion.6), channel_id=1, replica_groups=mesh['groups'=2,'row'=4,'col'=2,'tok'=2] {'col'}, use_global_device_ids=true, to_apply=%region_2.3 | all-reduce | flops 4096 | bytes 32768 | tf_op jit(solution)/shard_map/psum | solution.py:21
  157.5 0.6 add_sqrt_fusion
Async XLA Ops:
  6.5 34.3 %all-gather.2.cloned.1.call-start = ((), (), s32[]{:S(2)}) async-start(), calls=%async_computation.1 | async-start | bytes 2359296 | tf_op jit(solution)/shard_map/all_gather | solution.py:13
  7.3 137.3 %reduce-scatter.2.cloned.1.call-start = ((), (), s32[]{:S(2)}) async-start(), calls=%async_computation.2 | async-start | bytes 6291456 | tf_op jit(solution)/shard_map/reduce_scatter | solution.py:18
  40.9 23.5 %copy-start = (bf16[256,4096]{1,0:T(8,128)(2,1)S(1)}, bf16[256,4096]{1,0:T(8,128)(2,1)}, u32[]{:S(2)}) copy-start(bf16[256,4096]{1,0:T(8,128)(2,1)} %all-gather.2.cloned.1.call-done) | copy-start | bytes 6291460
Sparse Core Ops, SparseCore 0:
  9.0 31.7 all-gather.1
  90.7 53.7 reduce-scatter.1
where the time goes:
time: 165 us
  waiting for transfers between devices  87.4 us (53%)
  matrix products  26.2 us (16%)
  local copies, waits for them, and re-layouts  23.6 us (14%)
  between operations  13.4 us (8%)
  other arithmetic  7.26 us (4%)
  blocking collectives  6.99 us (4%)
    reduce_scatter x1, waiting for transfers between devices, per_device(): lax.psum_scatter(partial_value, 'col', scatter_dimension=0, tiled=True)  53.9 us
    all_gather x1, waiting for transfers between devices, per_device(): lax.all_gather(tokens, ('row', 'tok'), axis=0, tiled=True)  32.8 us
    dot_general x1, matrix products, per_device(): jnp.dot(lax.all_gather(tokens, ('row', 'tok'), axis=0, tiled=True), maske...  26.2 us
    broadcast_in_dim x1, local copies, waits for them, and re-layouts, per_device(): jnp.repeat(jnp.repeat(block_mask > 0, BLOCK, axis=0), BLOCK, axis=1)  23.4 us
    psum x1, blocking collectives, per_device(): totals = lax.psum(local_sums, 'col')  6.99 us
    reduce_sum x1, other arithmetic, per_device(): local_sums = jnp.sum(activated * activated, axis=0)  5.92 us
  transfers between devices with their start and end apart: 2, of which 2 were waited for; matrix products, arithmetic and copies ran while one was open for 0% of the time, Pallas kernels for 0%

commit v1 on v0

--- a/solution.py
+++ b/solution.py
@@ -1,9 +1,16 @@
+import functools
+
 import jax
 import jax.numpy as jnp
 from jax import lax
+from jax.experimental import pallas as pl
+from jax.experimental.pallas import tpu as pltpu
 from jax.sharding import PartitionSpec as P
 
 BLOCK = 128
+TILE = 512
+VMEM_CAP = 40 * 2**20
+MESH = pl.DeviceIdType.MESH
 
 
 def per_device(tokens, up_weight, block_mask):
@@ -22,14 +29,279 @@
     return jnp.sqrt(totals / token_count + 1e-06)
 
 
+def kernel(
+    rows, tile, tok_ref, w_hbm, mask_ref, out_ref,
+    w, toks, own, sent, sent_scale, got, got_scale, sums, sums_got,
+    w_sem, z_send, z_recv, p_send, p_recv, x_send, x_recv, s_send, s_recv, t_send, t_recv,
+):
+    r = lax.axis_index("row")
+    c = lax.axis_index("col")
+    k = lax.axis_index("tok")
+    held, depth = tok_ref.shape
+    width = w_hbm.shape[1]
+    tiles = width // tile
+    units = rows * tiles
+
+    def load(j):
+        return pltpu.make_async_copy(
+            w_hbm.at[:, pl.ds(pl.multiple_of(j * tile, tile), tile)], w.at[j], w_sem.at[j]
+        )
+
+    @pl.loop(0, tiles)
+    def _(j):
+        load(j).start()
+
+    barrier = pltpu.get_barrier_semaphore()
+    pl.semaphore_signal(barrier, inc=1, device_id={"tok": 1 - k}, device_id_type=MESH)
+    pl.semaphore_signal(barrier, inc=1, device_id={"col": 1 - c}, device_id_type=MESH)
+
+    @pl.when(r > 0)
+    def _():
+        pl.semaphore_signal(barrier, inc=1, device_id={"row": r - 1}, device_id_type=MESH)
+
+    @pl.when(r < rows - 1)
+    def _():
+        pl.semaphore_signal(barrier, inc=1, device_id={"row": r + 1}, device_id_type=MESH)
+
+    pl.semaphore_wait(barrier, 2 + jnp.minimum(r, 1) + jnp.minimum(rows - 1 - r, 1))
+
+    def along(s, direction, from_input=False):
+        return pltpu.make_async_remote_copy(
+            src_ref=tok_ref if from_input else toks.at[s, k],
+            dst_ref=toks.at[s, k],
+            send_sem=z_send.at[direction, s],
+            recv_sem=z_recv.at[s],
+            device_id={"row": r + 2 * direction - 1},
+            device_id_type=MESH,
+        )
+
+    def across(s, from_input=False):
+        return pltpu.make_async_remote_copy(
+            src_ref=tok_ref if from_input else toks.at[s, k],
+            dst_ref=toks.at[s, k],
+            send_sem=p_send.at[s],
+            recv_sem=p_recv.at[s],
+            device_id={"tok": 1 - k},
+            device_id_type=MESH,
+        )
+
+    def partials(u):
+        return pltpu.make_async_remote_copy(
+            src_ref=sent.at[u],
+            dst_ref=got.at[u],
+            send_sem=x_send.at[u],
+            recv_sem=x_recv.at[u],
+            device_id={"col": 1 - c},
+            device_id_type=MESH,
+        )
+
+    def scales(u):
+        return pltpu.make_async_remote_copy(
+            src_ref=sent_scale.at[u],
+            dst_ref=got_scale.at[u],
+            send_sem=s_send.at[u],
+            recv_sem=s_recv.at[u],
+            device_id={"col": 1 - c},
+            device_id_type=MESH,
+        )
+
+    across(r, True).start()
+
+    @pl.when(r > 0)
+    def _():
+        along(r, 0, True).start()
+
+    @pl.when(r < rows - 1)
+    def _():
+        along(r, 1, True).start()
+
+    toks[r, k] = tok_ref[...]
+    sums[...] = jnp.zeros_like(sums)
+
+    def forward(d):
+        @pl.when(r - d >= 0)
+        def _():
+            s = r - d
+            along(s, 1).wait_recv()
+
+            @pl.when(r < rows - 1)
+            def _():
+                along(s, 1).start()
+
+            across(s).start()
+
+        @pl.when(r + d < rows)
+        def _():
+            s = r + d
+            along(s, 0).wait_recv()
+
+            @pl.when(r > 0)
+            def _():
+                along(s, 0).start()
+
+            across(s).start()
+
+    near = jnp.minimum(r, rows - 1 - r)
+
+    def source(p):
+        d = (p + 1) // 2
+        paired = jnp.where(p % 2 == 1, r - d, r + d)
+        return jnp.where(p <= 2 * near, paired, jnp.where(2 * r < rows - 1, p, rows - 1 - p))
+
+    def finish(u):
+        j = u % tiles
+        partials(u).wait_recv()
+        scales(u).wait_recv()
+        theirs = got[u].astype(jnp.int32).astype(jnp.float32) * got_scale[u]
+        v = own[u] + theirs
+        a = 0.5 * v * (1.0 + lax.erf(v * (0.5**0.5)))
+        sums[j] += jnp.sum(a * a, axis=0, keepdims=True)
+
+    def unit(u, carry):
+        p = u // tiles
+        j = u % tiles
+        s = source(p)
+
+        @pl.when(p == 0)
+        def _():
+            load(j).wait()
+
+            @pl.loop(0, depth // BLOCK)
+            def _(i):
+                at = pl.ds(pl.multiple_of(i * BLOCK, BLOCK), BLOCK)
+                for b in range(tile // BLOCK):
+                    keep = (mask_ref[i, j * (tile // BLOCK) + b] > 0).astype(jnp.float32)
+                    cols = slice(b * BLOCK, (b + 1) * BLOCK)
+                    w[j, at, cols] = w[j, at, cols] * jnp.full((BLOCK, BLOCK), keep).astype(jnp.bfloat16)
+
+        @pl.when(jnp.logical_and(j == tiles // 2, p < rows - 1))
+        def _():
+            forward(p + 1)
+
+        @pl.when(j == 0)
+        def _():
+            across(s).wait_recv()
+
+        pre = jnp.dot(
+            toks[s].reshape(2 * held, depth), w[j], preferred_element_type=jnp.float32
+        )
+        own[u] = jnp.where(c == 0, pre[:held], pre[held:])
+        other = jnp.where(c == 0, pre[held:], pre[:held])
+        top = jnp.maximum(jnp.max(jnp.abs(other), axis=0, keepdims=True), 1e-30)
+        sent_scale[u] = top * (1.0 / 32766.0)
+        sent[u] = jnp.round(other * (32766.0 / top)).astype(jnp.int32).astype(jnp.int16)
+        partials(u).start()
+        scales(u).start()
+
+        @pl.when(u >= tiles)
+        def _():
+            finish(u - tiles)
+
+        return carry
+
+    lax.fori_loop(0, units, unit, 0)
+
+    @pl.loop(units - tiles, units)
+    def _(u):
+        finish(u)
+
+    total = pltpu.make_async_remote_copy(
+        src_ref=sums,
+        dst_ref=sums_got,
+        send_sem=t_send,
+        recv_sem=t_recv,
+        device_id={"col": 1 - c},
+        device_id_type=MESH,
+    )
+    total.start()
+
+    @pl.loop(0, units)
+    def _(u):
+        partials(u).wait_send()
+        scales(u).wait_send()
+
+    @pl.loop(0, rows)
+    def _(s):
+        across(s).wait_send()
+
+        @pl.when(jnp.logical_and(s <= r, r < rows - 1))
+        def _():
+            along(s, 1).wait_send()
+
+        @pl.when(jnp.logical_and(s >= r, r > 0))
+        def _():
+            along(s, 0).wait_send()
+
+    total.wait()
+    count = rows * 2 * held
+    out_ref[...] = jnp.sqrt((sums[...] + sums_got[...]) / count + 1e-06)
+
+
+def fused(rows, tokens, up_weight, block_mask):
+    held, depth = tokens.shape
+    width = up_weight.shape[1]
+    tile = min(TILE, width)
+    tiles = width // tile
+    units = rows * tiles
+    dma = pltpu.SemaphoreType.DMA
+    out = pl.pallas_call(
+        functools.partial(kernel, rows, tile),
+        out_shape=jax.ShapeDtypeStruct((tiles, 1, tile), jnp.float32),
+        in_specs=[
+            pl.BlockSpec(memory_space=pltpu.VMEM),
+            pl.BlockSpec(memory_space=pl.ANY),
+            pl.BlockSpec(memory_space=pltpu.SMEM),
+        ],
+        out_specs=pl.BlockSpec(memory_space=pltpu.VMEM),
+        scratch_shapes=[
+            pltpu.VMEM((tiles, depth, tile), jnp.bfloat16),
+            pltpu.VMEM((rows, 2, held, depth), jnp.bfloat16),
+            pltpu.VMEM((units, held, tile), jnp.float32),
+            pltpu.VMEM((units, held, tile), jnp.int16),
+            pltpu.VMEM((units, 1, tile), jnp.float32),
+            pltpu.VMEM((units, held, tile), jnp.int16),
+            pltpu.VMEM((units, 1, tile), jnp.float32),
+            pltpu.VMEM((tiles, 1, tile), jnp.float32),
+            pltpu.VMEM((tiles, 1, tile), jnp.float32),
+            dma((tiles,)),
+            dma((2, rows)),
+            dma((rows,)),
+            dma((rows,)),
+            dma((rows,)),
+            dma((units,)),
+            dma((units,)),
+            dma((units,)),
+            dma((units,)),
+            dma,
+            dma,
+        ],
+        compiler_params=pltpu.CompilerParams(
+            collective_id=0, has_side_effects=True, vmem_limit_bytes=56 * 2**20
+        ),
+    )(tokens, up_weight, block_mask)
+    return out.reshape(width)
+
+
 def solution(mesh):
     placed = (
         P(("groups", "row", "tok"), "col"),
         P("col", ("row", "tok")),
         P("col", ("row", "tok")),
     )
+    rows = mesh.shape["row"]
+    pairs = mesh.shape["col"] == 2 and mesh.shape["tok"] == 2 and rows > 1
+
+    def body(tokens, up_weight, block_mask):
+        held, depth = tokens.shape
+        width = up_weight.shape[1]
+        fits = up_weight.size * 2 <= VMEM_CAP and held % 16 == 0
+        fits = fits and depth % BLOCK == 0 and width % min(TILE, width) == 0
+        if pairs and fits:
+            return fused(rows, tokens, up_weight, block_mask)
+        return per_device(tokens, up_weight, block_mask)
+
     return jax.shard_map(
-        per_device,
+        body,
         mesh=mesh,
         in_specs=placed,
         out_specs=P(("groups", "row", "tok")),

time: 165 us -> 53.4 us (0.32)
  waiting for transfers between devices: 87.4 us -> 0 us
  Pallas kernels: 0 us -> 51.7 us
  matrix products: 26.2 us -> 0 us
  local copies, waits for them, and re-layouts: 23.6 us -> 1.32 us
  between operations: 13.4 us -> 0.01 us
  other arithmetic: 7.26 us -> 0 us
  blocking collectives: 6.99 us -> 0 us
    reduce_scatter x1 -> x0, waiting for transfers between devices: 53.9 us -> none  [per_device(): lax.psum_scatter(partial_value, 'col', scatter_dimension=0, tiled=True)]
    pallas_call x0 -> x1, Pallas kernels: none -> 51.7 us  [fused(): pl.pallas_call(functools.partial(kernel, rows, tile), out_shape=jax.Shape...]
    all_gather x1 -> x0, waiting for transfers between devices: 32.8 us -> none  [per_device(): lax.all_gather(tokens, ('row', 'tok'), axis=0, tiled=True)]
    dot_general x1 -> x0, matrix products: 26.2 us -> none  [per_device(): jnp.dot(lax.all_gather(tokens, ('row', 'tok'), axis=0, tiled=True), maske...]
    broadcast_in_dim x2 -> x0, local copies, waits for them, and re-layouts: 23.6 us -> none  [the longest x1 23.4 us: per_device(): jnp.repeat(jnp.repeat(block_mask > 0, BLOCK, axis=0), BLOCK, axis=1)]
    psum x1 -> x0, blocking collectives: 6.99 us -> none  [per_device(): totals = lax.psum(local_sums, 'col')]
    reduce_sum x1 -> x0, other arithmetic: 5.92 us -> none  [per_device(): local_sums = jnp.sum(activated * activated, axis=0)]
  transfers between devices with their start and end apart: 2 -> 0, of which waited for: 2 -> 0; matrix products, arithmetic and copies ran while one was open for 0% -> 0% of each run, Pallas kernels for 0% -> 0%
where the time goes in v1:
time: 53.4 us; the launch traced here: 53.1 us
  Pallas kernels  51.7 us (97%)
  local copies, waits for them, and re-layouts  1.32 us (2%)
    pallas_call x1, Pallas kernels, fused(): pl.pallas_call(functools.partial(kernel, rows, tile), out_shape=jax.Shape...  51.7 us
    unnamed x1, local copies, waits for them, and re-layouts  1.32 us

profile of v1, /device:TPU:0, one launch (start us, length us, event | category | flops | bytes accessed | tf_op | source)
XLA Modules:
  0.0 53.1 jit_solution(9776961215308083148)
XLA Ops:
  0.0 51.7 %shard_map.37 = f32[8,1,512]{2,1,0:T(1,128)} custom-call(bf16[32,4096]{1,0:T(8,128)(2,1)} %tok_ref.1, bf16[4096,4096]{1,0:T(8,128)(2,1)} %w_hbm.1, s32[32,32]{1,0:T(8,128)} %mask_ref.1), custom_call_target="tpu_custom_call" | custom-call | tf_op jit(solution)/shard_map/pallas_call | solution.py:247
  51.7 1.3 %copy.5 = f32[4096]{0:T(1024)} copy(f32[4096]{0:T(1024)} %bitcast.1) | data formatting | bytes 32768

commit v2 on v1

--- a/solution.py
+++ b/solution.py
@@ -9,6 +9,7 @@
 
 BLOCK = 128
 TILE = 512
+EARLY = 4
 VMEM_CAP = 40 * 2**20
 MESH = pl.DeviceIdType.MESH
 
@@ -41,6 +42,7 @@
     width = w_hbm.shape[1]
     tiles = width // tile
     units = rows * tiles
+    early = min(EARLY, tiles)
 
     def load(j):
         return pltpu.make_async_copy(
@@ -157,34 +159,28 @@
         a = 0.5 * v * (1.0 + lax.erf(v * (0.5**0.5)))
         sums[j] += jnp.sum(a * a, axis=0, keepdims=True)
 
-    def unit(u, carry):
-        p = u // tiles
-        j = u % tiles
-        s = source(p)
-
-        @pl.when(p == 0)
-        def _():
-            load(j).wait()
-
-            @pl.loop(0, depth // BLOCK)
-            def _(i):
-                at = pl.ds(pl.multiple_of(i * BLOCK, BLOCK), BLOCK)
+    def dot(x, j):
+        total = None
+        for i in range(0, depth // BLOCK, 2):
+            blocks = []
+            for h in range(i, i + 2):
+                line = []
                 for b in range(tile // BLOCK):
-                    keep = (mask_ref[i, j * (tile // BLOCK) + b] > 0).astype(jnp.float32)
-                    cols = slice(b * BLOCK, (b + 1) * BLOCK)
-                    w[j, at, cols] = w[j, at, cols] * jnp.full((BLOCK, BLOCK), keep).astype(jnp.bfloat16)
-
-        @pl.when(jnp.logical_and(j == tiles // 2, p < rows - 1))
-        def _():
-            forward(p + 1)
-
-        @pl.when(j == 0)
-        def _():
-            across(s).wait_recv()
-
-        pre = jnp.dot(
-            toks[s].reshape(2 * held, depth), w[j], preferred_element_type=jnp.float32
-        )
+                    keep = (mask_ref[h, j * (tile // BLOCK) + b] > 0).astype(jnp.float32)
+                    keep = jnp.full((BLOCK, BLOCK), keep).astype(jnp.bfloat16)
+                    line.append(
+                        w[j, h * BLOCK : (h + 1) * BLOCK, b * BLOCK : (b + 1) * BLOCK] * keep
+                    )
+                blocks.append(jnp.concatenate(line, axis=1))
+            part = jnp.dot(
+                x[:, i * BLOCK : (i + 2) * BLOCK],
+                jnp.concatenate(blocks, axis=0),
+                preferred_element_type=jnp.float32,
+            )
+            total = part if total is None else total + part
+        return total
+
+    def emit(u, pre):
         own[u] = jnp.where(c == 0, pre[:held], pre[held:])
         other = jnp.where(c == 0, pre[held:], pre[:held])
         top = jnp.maximum(jnp.max(jnp.abs(other), axis=0, keepdims=True), 1e-30)
@@ -193,17 +189,70 @@
         partials(u).start()
         scales(u).start()
 
-        @pl.when(u >= tiles)
-        def _():
-            finish(u - tiles)
-
-        return carry
-
-    lax.fori_loop(0, units, unit, 0)
-
-    @pl.loop(units - tiles, units)
-    def _(u):
-        finish(u)
+    def chunk(p):
+        return toks[source(p)].reshape(2 * held, depth)
+
+    def single(p, j):
+        emit(p * tiles + j, dot(chunk(p), j))
+
+        @pl.when(p >= 2)
+        def _():
+            finish((p - 2) * tiles + j)
+
+    def double(p, j):
+        pre = dot(jnp.concatenate([chunk(p), chunk(p + 1)], axis=0), j)
+        emit(p * tiles + j, pre[: 2 * held])
+        emit((p + 1) * tiles + j, pre[2 * held :])
+
+        @pl.when(p >= 2)
+        def _():
+            finish((p - 2) * tiles + j)
+            finish((p - 1) * tiles + j)
+
+    @pl.loop(0, rows // 2)
+    def _(q):
+        p = 2 * q
+        across(source(p)).wait_recv()
+
+        @pl.loop(0, early)
+        def _(j):
+            @pl.when(q == 0)
+            def _():
+                load(j).wait()
+
+            single(p, j)
+
+        forward(p + 1)
+        across(source(p + 1)).wait_recv()
+
+        @pl.loop(early, tiles)
+        def _(j):
+            @pl.when(q == 0)
+            def _():
+                load(j).wait()
+
+            double(p, j)
+
+        @pl.loop(0, early)
+        def _(j):
+            @pl.when(jnp.logical_and(j == early // 2, p + 2 < rows))
+            def _():
+                forward(p + 2)
+
+            single(p + 1, j)
+
+    @pl.loop(0, early)
+    def _(j):
+        finish((rows - 2) * tiles + j)
+
+    @pl.loop(early, tiles)
+    def _(j):
+        finish((rows - 2) * tiles + j)
+        finish((rows - 1) * tiles + j)
+
+    @pl.loop(0, early)
+    def _(j):
+        finish((rows - 1) * tiles + j)
 
     total = pltpu.make_async_remote_copy(
         src_ref=sums,
@@ -289,13 +338,13 @@
         P("col", ("row", "tok")),
     )
     rows = mesh.shape["row"]
-    pairs = mesh.shape["col"] == 2 and mesh.shape["tok"] == 2 and rows > 1
+    pairs = mesh.shape["col"] == 2 and mesh.shape["tok"] == 2 and rows % 2 == 0
 
     def body(tokens, up_weight, block_mask):
         held, depth = tokens.shape
         width = up_weight.shape[1]
         fits = up_weight.size * 2 <= VMEM_CAP and held % 16 == 0
-        fits = fits and depth % BLOCK == 0 and width % min(TILE, width) == 0
+        fits = fits and depth % (2 * BLOCK) == 0 and width % min(TILE, width) == 0
         if pairs and fits:
             return fused(rows, tokens, up_weight, block_mask)
         return per_device(tokens, up_weight, block_mask)

time: 53.4 us -> 43.3 us (0.81)
  Pallas kernels: 51.7 us -> 41.7 us
    pallas_call x1, Pallas kernels: 51.7 us -> 41.7 us  [fused(): pl.pallas_call(functools.partial(kernel, rows, tile), out_shape=jax.Shape...]
where the time goes in v2:
time: 43.3 us; the launch traced here: 43 us
  Pallas kernels  41.7 us (96%)
  local copies, waits for them, and re-layouts  1.32 us (3%)
    pallas_call x1, Pallas kernels, fused(): pl.pallas_call(functools.partial(kernel, rows, tile), out_shape=jax.Shape...  41.7 us
    unnamed x1, local copies, waits for them, and re-layouts  1.32 us

profile of v2, /device:TPU:0, one launch (start us, length us, event | category | flops | bytes accessed | tf_op | source)
XLA Modules:
  0.0 43.0 jit_solution(16617358552112303867)
XLA Ops:
  0.0 41.7 %shard_map.37 = f32[8,1,512]{2,1,0:T(1,128)} custom-call(bf16[32,4096]{1,0:T(8,128)(2,1)} %tok_ref.1, bf16[4096,4096]{1,0:T(8,128)(2,1)} %w_hbm.1, s32[32,32]{1,0:T(8,128)} %mask_ref.1), custom_call_target="tpu_custom_call" | custom-call | tf_op jit(solution)/shard_map/pallas_call | solution.py:296
  41.7 1.3 %copy.5 = f32[4096]{0:T(1024)} copy(f32[4096]{0:T(1024)} %bitcast.1) | data formatting | bytes 32768

commit v3 on v2

--- a/solution.py
+++ b/solution.py
@@ -42,7 +42,7 @@
     width = w_hbm.shape[1]
     tiles = width // tile
     units = rows * tiles
-    early = min(EARLY, tiles)
+    early = min(EARLY, tiles - 1)
 
     def load(j):
         return pltpu.make_async_copy(
@@ -67,22 +67,25 @@
 
     pl.semaphore_wait(barrier, 2 + jnp.minimum(r, 1) + jnp.minimum(rows - 1 - r, 1))
 
-    def along(s, direction, from_input=False):
+    def half(h):
+        return slice(h * (depth // 2), (h + 1) * (depth // 2))
+
+    def along(s, direction, h, from_input=False):
         return pltpu.make_async_remote_copy(
-            src_ref=tok_ref if from_input else toks.at[s, k],
-            dst_ref=toks.at[s, k],
-            send_sem=z_send.at[direction, s],
-            recv_sem=z_recv.at[s],
+            src_ref=tok_ref.at[:, half(h)] if from_input else toks.at[s, k, :, half(h)],
+            dst_ref=toks.at[s, k, :, half(h)],
+            send_sem=z_send.at[direction, h, s],
+            recv_sem=z_recv.at[h, s],
             device_id={"row": r + 2 * direction - 1},
             device_id_type=MESH,
         )
 
-    def across(s, from_input=False):
+    def across(s, h, from_input=False):
         return pltpu.make_async_remote_copy(
-            src_ref=tok_ref if from_input else toks.at[s, k],
-            dst_ref=toks.at[s, k],
-            send_sem=p_send.at[s],
-            recv_sem=p_recv.at[s],
+            src_ref=tok_ref.at[:, half(h)] if from_input else toks.at[s, k, :, half(h)],
+            dst_ref=toks.at[s, k, :, half(h)],
+            send_sem=p_send.at[h, s],
+            recv_sem=p_recv.at[h, s],
             device_id={"tok": 1 - k},
             device_id_type=MESH,
         )
@@ -107,41 +110,44 @@
             device_id_type=MESH,
         )
 
-    across(r, True).start()
+    for h in range(2):
+        across(r, h, True).start()
 
     @pl.when(r > 0)
     def _():
-        along(r, 0, True).start()
+        for h in range(2):
+            along(r, 0, h, True).start()
 
     @pl.when(r < rows - 1)
     def _():
-        along(r, 1, True).start()
+        for h in range(2):
+            along(r, 1, h, True).start()
 
     toks[r, k] = tok_ref[...]
     sums[...] = jnp.zeros_like(sums)
 
-    def forward(d):
+    def forward(d, h):
         @pl.when(r - d >= 0)
         def _():
             s = r - d
-            along(s, 1).wait_recv()
+            along(s, 1, h).wait_recv()
 
             @pl.when(r < rows - 1)
             def _():
-                along(s, 1).start()
-
-            across(s).start()
+                along(s, 1, h).start()
+
+            across(s, h).start()
 
         @pl.when(r + d < rows)
         def _():
             s = r + d
-            along(s, 0).wait_recv()
+            along(s, 0, h).wait_recv()
 
             @pl.when(r > 0)
             def _():
-                along(s, 0).start()
-
-            across(s).start()
+                along(s, 0, h).start()
+
+            across(s, h).start()
 
     near = jnp.minimum(r, rows - 1 - r)
 
@@ -192,57 +198,55 @@
     def chunk(p):
         return toks[source(p)].reshape(2 * held, depth)
 
-    def single(p, j):
-        emit(p * tiles + j, dot(chunk(p), j))
-
-        @pl.when(p >= 2)
-        def _():
-            finish((p - 2) * tiles + j)
+    def arrive(p):
+        for h in range(2):
+            across(source(p), h).wait_recv()
 
     def double(p, j):
         pre = dot(jnp.concatenate([chunk(p), chunk(p + 1)], axis=0), j)
         emit(p * tiles + j, pre[: 2 * held])
         emit((p + 1) * tiles + j, pre[2 * held :])
 
-        @pl.when(p >= 2)
-        def _():
-            finish((p - 2) * tiles + j)
-            finish((p - 1) * tiles + j)
-
-    @pl.loop(0, rows // 2)
-    def _(q):
-        p = 2 * q
-        across(source(p)).wait_recv()
-
-        @pl.loop(0, early)
+    arrive(0)
+
+    @pl.loop(0, early)
+    def _(j):
+        load(j).wait()
+        emit(j, dot(chunk(0), j))
+
+    forward(1, 0)
+
+    @pl.loop(0, rows - 1)
+    def _(p):
+        forward(p + 1, 1)
+        arrive(p + 1)
+        low = jnp.where(p % 2 == 0, early, 0)
+        high = jnp.where(p % 2 == 0, tiles, early)
+
+        @pl.loop(low, high)
         def _(j):
-            @pl.when(q == 0)
+            @pl.when(p == 0)
             def _():
                 load(j).wait()
 
-            single(p, j)
-
-        forward(p + 1)
-        across(source(p + 1)).wait_recv()
-
-        @pl.loop(early, tiles)
-        def _(j):
-            @pl.when(q == 0)
-            def _():
-                load(j).wait()
+            @pl.when(jnp.logical_and(j == high - 1, p + 2 < rows))
+            def _():
+                forward(p + 2, 0)
 
             double(p, j)
 
-        @pl.loop(0, early)
-        def _(j):
-            @pl.when(jnp.logical_and(j == early // 2, p + 2 < rows))
-            def _():
-                forward(p + 2)
-
-            single(p + 1, j)
+            @pl.when(p >= 2)
+            def _():
+                finish((p - 2) * tiles + j)
+
+            @pl.when(p >= 1)
+            def _():
+                finish((p - 1) * tiles + j)
 
     @pl.loop(0, early)
     def _(j):
+        emit((rows - 1) * tiles + j, dot(chunk(rows - 1), j))
+        finish((rows - 3) * tiles + j)
         finish((rows - 2) * tiles + j)
 
     @pl.loop(early, tiles)
@@ -271,15 +275,18 @@
 
     @pl.loop(0, rows)
     def _(s):
-        across(s).wait_send()
+        for h in range(2):
+            across(s, h).wait_send()
 
         @pl.when(jnp.logical_and(s <= r, r < rows - 1))
         def _():
-            along(s, 1).wait_send()
+            for h in range(2):
+                along(s, 1, h).wait_send()
 
         @pl.when(jnp.logical_and(s >= r, r > 0))
         def _():
-            along(s, 0).wait_send()
+            for h in range(2):
+                along(s, 0, h).wait_send()
 
     total.wait()
     count = rows * 2 * held
@@ -289,7 +296,7 @@
 def fused(rows, tokens, up_weight, block_mask):
     held, depth = tokens.shape
     width = up_weight.shape[1]
-    tile = min(TILE, width)
+    tile = TILE
     tiles = width // tile
     units = rows * tiles
     dma = pltpu.SemaphoreType.DMA
@@ -313,10 +320,10 @@
             pltpu.VMEM((tiles, 1, tile), jnp.float32),
             pltpu.VMEM((tiles, 1, tile), jnp.float32),
             dma((tiles,)),
+            dma((2, 2, rows)),
             dma((2, rows)),
-            dma((rows,)),
-            dma((rows,)),
-            dma((rows,)),
+            dma((2, rows)),
+            dma((2, rows)),
             dma((units,)),
             dma((units,)),
             dma((units,)),
@@ -338,13 +345,13 @@
         P("col", ("row", "tok")),
     )
     rows = mesh.shape["row"]
-    pairs = mesh.shape["col"] == 2 and mesh.shape["tok"] == 2 and rows % 2 == 0
+    pairs = mesh.shape["col"] == 2 and mesh.shape["tok"] == 2 and rows % 2 == 0 and rows > 2
 
     def body(tokens, up_weight, block_mask):
         held, depth = tokens.shape
         width = up_weight.shape[1]
         fits = up_weight.size * 2 <= VMEM_CAP and held % 16 == 0
-        fits = fits and depth % (2 * BLOCK) == 0 and width % min(TILE, width) == 0
+        fits = fits and depth % (2 * BLOCK) == 0 and width % TILE == 0 and width > TILE
         if pairs and fits:
             return fused(rows, tokens, up_weight, block_mask)
         return per_device(tokens, up_weight, block_mask)

time: 43.3 us -> 42.4 us (0.979)
  Pallas kernels: 41.7 us -> 40.8 us
    pallas_call x1, Pallas kernels: 41.7 us -> 40.8 us  [fused(): pl.pallas_call(functools.partial(kernel, rows, tile), out_shape=jax.Shape...]
where the time goes in v3:
time: 42.4 us; the launch traced here: 42.1 us
  Pallas kernels  40.8 us (96%)
  local copies, waits for them, and re-layouts  1.32 us (3%)
    pallas_call x1, Pallas kernels, fused(): pl.pallas_call(functools.partial(kernel, rows, tile), out_shape=jax.Shape...  40.8 us
    unnamed x1, local copies, waits for them, and re-layouts  1.32 us

profile of v3, /device:TPU:0, one launch (start us, length us, event | category | flops | bytes accessed | tf_op | source)
XLA Modules:
  0.0 42.1 jit_solution(4039590078841538081)
XLA Ops:
  0.0 40.8 %shard_map.37 = f32[8,1,512]{2,1,0:T(1,128)} custom-call(bf16[32,4096]{1,0:T(8,128)(2,1)} %tok_ref.1, bf16[4096,4096]{1,0:T(8,128)(2,1)} %w_hbm.1, s32[32,32]{1,0:T(8,128)} %mask_ref.1), custom_call_target="tpu_custom_call" | custom-call | tf_op jit(solution)/shard_map/pallas_call | solution.py:303
  40.8 1.3 %copy.5 = f32[4096]{0:T(1024)} copy(f32[4096]{0:T(1024)} %bitcast.1) | data formatting | bytes 32768
